TPU v7x, 256 devices: a whole 4x4x8 slice. The times are simulated.
256 devices in a mesh: dp: 16 (over y_lo, z), proto: 16 (over x, y_hi, core).
Axes of the slice: x: 4, y: 4 (y_hi: 2, y_lo: 2; y = y_hi * 2 + y_lo), z: 8, core: 2. Of those that a mesh axis runs over, the one named last changes fastest.
Arguments:
- student_feats: bfloat16 [16384, 256], P('dp'), may hold values from -0.5 to 0.5
- teacher_feats: bfloat16 [16384, 256], P('dp'), may hold values from -6 to 6
- student_protos: bfloat16 [256, 65536], P(None, 'proto'), may hold values from -0.375 to 0.375
- teacher_protos: bfloat16 [256, 65536], P(None, 'proto'), may hold values from -0.1875 to 0.1875
Outputs:
- proto_grad: float32 [256, 65536], P(None, 'proto')
- feature_grad: float32 [16384, 256], P('dp')
All inputs are finite; a program needn't handle non-finite values.
Results may differ from a plain program's by a relative error of at most 0.0009.
The roundings to bfloat16 on the way count: a program that leaves them out, or rounds other values in their place, can miss the bound.
Values sent between devices are 32-bit elements; how exact they have to be, the bound alone decides.
A program may use at most 128 MiB of HBM per device.

v0:
```python
import functools
import math

import jax
import jax.numpy as jnp
from jax import lax
from jax.experimental import pallas as pl
from jax.experimental.pallas import tpu as pltpu
from jax.sharding import PartitionSpec as P

PROTOS = 65536
ROUNDS = 3
EPS = 1e-06
TEACHER_TEMP = 0.07
STUDENT_TEMP = 0.1
LOG2E = 1.4426950408889634
MESH = pl.DeviceIdType.MESH
F32 = jnp.float32
BF16 = jnp.bfloat16


def unit_rows(values):
    wide = values.astype(F32)
    norms = jnp.sqrt(jnp.sum(wide * wide, axis=1, keepdims=True) + EPS)
    return (wide * (1.0 / norms), norms)


def unit_cols(values):
    wide = values.astype(F32)
    norms = jnp.sqrt(jnp.sum(wide * wide, axis=0, keepdims=True) + EPS)
    return (wide * (1.0 / norms), norms)


def wait_bytes(ref, sem):
    pltpu.make_async_copy(ref, ref, sem).wait()


def kernel(
    n_dp, n_pr,
    sf_in, tf_in, sp_in, tp_in,
    pg_ref, fg_ref,
    sf_ref, tf_ref, sp_ref, tp_ref, wts,
    expo, th, sh, part, vb, ub, racc, first,
    csend, crecv, rsend, rrecv,
    st, wsn, pb, gbuf, hat, ubuf, yrecv, zrecv, brecv, gat, h1, h2, h3,
    csend_sem, crecv_sem, rsend_sem, rrecv_sem,
    ysend_sem, yrecv_sem, zsend_sem, zrecv_sem, bsend_sem, brecv_sem,
    gzsend_sem, gzrecv_sem, gysend_sem, gyrecv_sem, hsend_sem, hrecv_sem, in_sem,
):
    rows, dim = sf_ref.shape
    cols = tp_ref.shape[1]
    me = lax.axis_index("dp")
    mp = lax.axis_index("proto")
    width = cols // n_dp
    blocks = rows // 128
    nz = n_dp // 2
    y, z = me // nz, lax.rem(me, nz)
    other = {"dp": (1 - y) * nz + z}
    sides = ({"dp": y * nz + lax.rem(z + 1, nz)}, {"dp": y * nz + lax.rem(z + nz - 1, nz)})
    part_rows = dim // 4
    core, h, x = lax.rem(mp, 2), lax.rem(mp // 2, 2), mp // 4
    nx = n_pr // 4
    factor = PROTOS / math.sqrt(rows * n_dp) / STUDENT_TEMP

    def peer(nx_, nh, ncore):
        return {"proto": (nx_ * 2 + nh) * 2 + ncore}

    loads = [
        pltpu.make_async_copy(src, dst, in_sem.at[k])
        for k, (src, dst) in enumerate(((tf_in, tf_ref), (tp_in, tp_ref), (sf_in, sf_ref), (sp_in, sp_ref)))
    ]
    for load in loads:
        load.start()
    barrier = pltpu.get_barrier_semaphore()

    def greet_dp(j, _):
        pl.semaphore_signal(barrier, inc=1, device_id={"dp": lax.rem(me + j, n_dp)}, device_id_type=MESH)
        return 0

    def greet_pr(j, _):
        pl.semaphore_signal(barrier, inc=1, device_id={"proto": lax.rem(mp + j, n_pr)}, device_id_type=MESH)
        return 0

    lax.fori_loop(1, n_dp, greet_dp, 0)
    lax.fori_loop(1, n_pr, greet_pr, 0)

    def norm_rows(b, _):
        r = pl.ds(pl.multiple_of(b * 128, 128), 128)
        th[r, :] = unit_rows(tf_ref[r, :])[0].astype(BF16)
        return 0

    def norm_student(b, _):
        r = pl.ds(pl.multiple_of(b * 128, 128), 128)
        unit = unit_rows(sf_ref[r, :])[0]
        sh[r, :] = unit.astype(BF16)
        turned = unit.T.astype(BF16)
        st[pl.ds(pl.multiple_of((1 - y) * part_rows, part_rows), part_rows), r] = turned[:part_rows]
        st[pl.ds(pl.multiple_of(y * part_rows, part_rows), part_rows), r] = turned[part_rows:2 * part_rows]
        st[2 * part_rows:, r] = turned[2 * part_rows:]
        return 0

    loads[0].wait()
    lax.fori_loop(0, blocks, norm_rows, 0)
    loads[1].wait()
    tiles = width // 128
    half_tiles = n_dp * tiles // 2

    def hops(j, n):
        return min(j, n - j)

    dp_peers = sorted(
        [(a, j) for a in range(2) for j in range(nz) if a or j],
        key=lambda o: -(o[0] + hops(o[1], nz)))
    pr_peers = sorted(
        [(i, b, c) for i in range(nx) for b in range(2) for c in range(2) if i or b or c],
        key=lambda o: -(2 * hops(o[0], nx) + 4 * o[1] + o[2]))

    def send_cols(rnd, hf):
        r = pl.ds(hf * half_tiles, half_tiles)
        for slot, (a, j) in enumerate(dp_peers):
            pltpu.make_async_remote_copy(
                src_ref=csend.at[rnd, r], dst_ref=crecv.at[rnd, hf, slot],
                send_sem=csend_sem.at[rnd, hf], recv_sem=crecv_sem.at[rnd, hf],
                device_id={"dp": lax.rem(y + a, 2) * nz + lax.rem(z + j, nz)}, device_id_type=MESH,
            ).start()

    def put_cols(rnd, k, sums):
        for t in range(tiles):
            csend[rnd, pl.ds(k * tiles + t, 1), :] = sums[:, t * 128:(t + 1) * 128]

    def teacher_unit(k):
        c = pl.ds(pl.multiple_of(k * width, width), width)
        return unit_cols(tp_ref[:, c])[0].astype(BF16)

    def first_cols(k, _):
        c = pl.ds(pl.multiple_of(k * width, width), width)
        wt = wts[lax.rem(k, 2)]
        wts[lax.rem(k + 1, 2)] = teacher_unit(jnp.minimum(k + 1, n_dp - 1))
        acc = jnp.zeros((8, width), F32)
        for m in range(rows // 256):
            r = pl.ds(m * 256, 256)
            logits = jnp.dot(th[r, :], wt, preferred_element_type=F32)
            e = jnp.exp2(logits * (LOG2E / TEACHER_TEMP))
            expo[r, c] = e
            acc = acc + jnp.sum(e.reshape(32, 8, width), axis=0)
        put_cols(0, k, jnp.sum(acc, axis=0, keepdims=True))
        return 0

    wts[0] = teacher_unit(0)
    lax.fori_loop(0, n_dp // 2, first_cols, 0, unroll=4)
    pl.semaphore_wait(barrier, n_dp + n_pr - 2)
    send_cols(0, 0)
    lax.fori_loop(n_dp // 2, n_dp, first_cols, 0, unroll=4)
    send_cols(0, 1)
    loads[2].wait()
    lax.fori_loop(0, blocks, norm_student, 0)
    loads[3].wait()

    part[...] = jnp.zeros_like(part)

    def student(lo, hi):
        def body(k, _):
            c = pl.ds(pl.multiple_of(k * width, width), width)
            ws = unit_cols(sp_ref[:, c])[0].astype(BF16)
            wsn[:, c] = ws
            for m in range(rows // 256):
                r = pl.ds(m * 256, 256)
                logits = jnp.dot(sh[r, :], ws, preferred_element_type=F32)
                e = jnp.exp2(logits * (LOG2E / STUDENT_TEMP))
                s = e[:, 0:128]
                for t in range(1, width // 128):
                    s = s + e[:, t * 128:(t + 1) * 128]
                part[r, :] += s
            return 0

        lax.fori_loop(lo, hi, body, 0)

    def receive_v(rnd, hf):
        wait_bytes(crecv.at[rnd, hf], crecv_sem.at[rnd, hf])
        v = 1.0 / (csend[rnd, pl.ds(hf * half_tiles, half_tiles), :] + jnp.sum(crecv[rnd, hf], axis=0))
        for t in range(half_tiles):
            lanes = slice((hf * half_tiles + t) * 128, (hf * half_tiles + t + 1) * 128)
            vb[:, lanes] = jnp.broadcast_to(v[t:t + 1, :], (8, 128))

    def lane_sums(slot, acc):
        for k in range(blocks):
            turned = acc[k * 128:(k + 1) * 128, :].T
            rsend[slot, k:k + 1, :] = jnp.sum(turned, axis=0, keepdims=True)

    def send_rows(slot):
        for place, (i, b, c) in enumerate(pr_peers):
            pltpu.make_async_remote_copy(
                src_ref=rsend.at[slot], dst_ref=rrecv.at[slot, place],
                send_sem=rsend_sem.at[slot], recv_sem=rrecv_sem.at[slot],
                device_id=peer(lax.rem(x + i, nx), lax.rem(h + b, 2), lax.rem(core + c, 2)), device_id_type=MESH,
            ).start()

    def receive_rows(slot):
        wait_bytes(rrecv.at[slot], rrecv_sem.at[slot])
        return 1.0 / (rsend[slot] + jnp.sum(rrecv[slot], axis=0))

    def widen(u, out):
        for k in range(blocks):
            out[k * 128:(k + 1) * 128, :] = jnp.broadcast_to(u[k:k + 1, :], (128, 128)).T

    def row_pass(rnd, hf):
        def body(k, _):
            r = pl.ds(pl.multiple_of(k * 128, 128), 128)
            acc = racc[r, :].reshape(16, 8, 128) if hf else jnp.zeros((16, 8, 128), F32)
            for t in range(hf * half_tiles, (hf + 1) * half_tiles):
                e = expo[r, t * 128:(t + 1) * 128].reshape(16, 8, 128)
                acc = acc + e * vb[:, t * 128:(t + 1) * 128][None]
            racc[r, :] = acc.reshape(128, 128)
            return 0

        lax.fori_loop(0, blocks, body, 0)
        if hf:
            lane_sums(rnd, racc)

    def col_pass(rnd, hf):
        def body(i, _):
            k = hf * (n_dp // 2) + i
            c = pl.ds(pl.multiple_of(k * width, width), width)

            def inner(b, acc):
                r = pl.ds(pl.multiple_of(b * 128, 128), 128)
                u = ub[r, :].reshape(16, 8, 128)
                e = expo[r, c].reshape(16, 8, width)
                new = [e[:, :, t * 128:(t + 1) * 128] * u for t in range(tiles)]
                return tuple(a + jnp.sum(n, axis=0) for a, n in zip(acc, new))

            acc = lax.fori_loop(0, blocks, inner, (jnp.zeros((8, 128), F32),) * tiles)
            put_cols(rnd, k, jnp.sum(jnp.concatenate(acc, axis=1), axis=0, keepdims=True))
            return 0

        lax.fori_loop(0, n_dp // 2, body, 0)

    def span(rel, hc):
        chunk = lax.rem(z + rel, nz)
        return pl.ds(pl.multiple_of((chunk * 2 + hc) * width, width), width)

    def place(b):
        q = b // 2
        far = nz // 2 - (q + 1) // 2
        return span(jnp.where(lax.rem(q, 2) == 1, far, nz - far), lax.rem(b, 2))

    def ready(b, _):
        ws = wsn[:, place(b)]
        for m in range(rows // 256):
            r = pl.ds(m * 256, 256)
            logits = jnp.dot(sh[r, :], ws, preferred_element_type=F32)
            e = jnp.exp2(logits * (LOG2E / STUDENT_TEMP)).reshape(32, 8, width)
            ps = pb[r, :].reshape(32, 8, 128)
            first[b, r, :] = jnp.concatenate(
                [e[:, :, t * 128:(t + 1) * 128] * ps for t in range(tiles)], axis=2).reshape(256, width)
        return 0

    share = n_dp // 4
    student(0, share)
    for rnd in range(ROUNDS):
        if rnd == 1:
            student(2 * share, 3 * share)
        receive_v(rnd, 0)
        row_pass(rnd, 0)
        receive_v(rnd, 1)
        row_pass(rnd, 1)
        send_rows(rnd)
        if rnd == 0:
            student(share, 2 * share)
        if rnd == 1:
            student(3 * share, 4 * share)

            lane_sums(ROUNDS, part)
            send_rows(ROUNDS)
        if rnd == ROUNDS - 1:
            widen(receive_rows(ROUNDS) * factor, pb)
            hat[...] = jnp.zeros_like(hat)
            lax.fori_loop(0, 2, ready, 0)
        u = receive_rows(rnd)
        if rnd < ROUNDS - 1:
            widen(u, ub)
            col_pass(rnd + 1, 0)
            send_cols(rnd + 1, 0)
            col_pass(rnd + 1, 1)
            send_cols(rnd + 1, 1)
        else:
            widen(u * factor, ub)
    def copy(src, dst, send, recv, to):
        return pltpu.make_async_remote_copy(
            src_ref=src, dst_ref=dst, send_sem=send, recv_sem=recv, device_id=to, device_id_type=MESH)

    def grad_block(b, _, made=False):
        c = place(b)
        ws = wsn[:, c]
        v = vb[:, c]
        for m in range(rows // 256):
            r = pl.ds(m * 256, 256)
            if made:
                e = first[b, r, :].reshape(32, 8, width)
            else:
                logits = jnp.dot(sh[r, :], ws, preferred_element_type=F32)
                e = jnp.exp2(logits * (LOG2E / STUDENT_TEMP)).reshape(32, 8, width)
            q = expo[r, c].reshape(32, 8, width)
            us = ub[r, :].reshape(32, 8, 128)
            ps = pb[r, :].reshape(32, 8, 128)
            g = []
            for t in range(tiles):
                lanes = slice(t * 128, (t + 1) * 128)
                p = e[:, :, lanes] if made else e[:, :, lanes] * ps
                g.append(p - q[:, :, lanes] * us * v[None, :, lanes])
            g = jnp.concatenate(g, axis=2).reshape(256, width).astype(BF16)
            gbuf[r, :] = g
            hat[r, :] += lax.dot_general(g, ws, (((1,), (1,)), ((), ())), preferred_element_type=F32)
        ubuf[b] = jnp.dot(st[...], gbuf[...], preferred_element_type=F32)
        copy(ubuf.at[b, pl.ds(0, part_rows)], yrecv.at[b], ysend_sem, yrecv_sem.at[b], other).start()
        return 0

    half_rows = rows // 2
    x_rows = half_rows // nx

    mine = pl.multiple_of(core * half_rows, half_rows)
    theirs = pl.multiple_of((1 - core) * half_rows, half_rows)

    def x_start(xx):
        return pl.multiple_of(xx * x_rows, x_rows)

    def hat_1():
        copy(hat.at[pl.ds(theirs, half_rows)], h1, hsend_sem.at[0], hrecv_sem.at[0], peer(x, h, 1 - core)).start()

    def hat_2():
        wait_bytes(h1, hrecv_sem.at[0])
        hat[pl.ds(mine, half_rows), :] += h1[...]
        for j in range(1, nx):
            to = lax.rem(x + j, nx)
            copy(hat.at[pl.ds(mine + x_start(to), x_rows)], h2.at[j - 1], hsend_sem.at[1], hrecv_sem.at[1],
                 peer(to, h, core)).start()

    def hat_3():
        wait_bytes(h2, hrecv_sem.at[1])
        h3[0] = hat[pl.ds(mine + x_start(x), x_rows), :] + jnp.sum(h2[...], axis=0)
        copy(h3.at[0], h3.at[1], hsend_sem.at[2], hrecv_sem.at[2], peer(x, 1 - h, core)).start()

    def hat_4():
        wait_bytes(h3.at[1], hrecv_sem.at[2])
        r = pl.ds(mine + x_start(x), x_rows)
        grad = h3[0] + h3[1]
        unit, norm = unit_rows(sf_ref[r, :])
        fg_ref[r, :] = (grad - unit * jnp.sum(unit * grad, axis=1, keepdims=True)) / norm
        for j in range(1, nx):
            copy(fg_ref.at[r], fg_ref.at[r], hsend_sem.at[3], hrecv_sem.at[3], peer(lax.rem(x + j, nx), h, core)).start()

    def hat_5():
        wait_bytes(h2, hrecv_sem.at[3])
        r = pl.ds(mine, half_rows)
        copy(fg_ref.at[r], fg_ref.at[r], hsend_sem.at[4], hrecv_sem.at[4], peer(x, h, 1 - core)).start()

    def hat_6():
        wait_bytes(h1, hrecv_sem.at[4])

    def piece_rows(p):
        return pl.ds((p + 1) * part_rows, part_rows)

    top = nz // 2

    def arrive(q, hc, p):
        b = 2 * q + hc
        block = ubuf[b, piece_rows(p)]
        if p == 0:
            wait_bytes(yrecv.at[b], yrecv_sem.at[b])
            block = block + yrecv[b]
        return block

    def landed(turn, t, hc, p):
        wait_bytes(zrecv.at[turn, t, hc, p], zrecv_sem.at[turn, t, hc, p])
        return zrecv[turn, t, hc, p]

    def ring(t, pieces, same=(True, False)):
        for p in pieces:
            for hc in range(2):
                for turn in range(2):
                    if (hc == turn) not in same or (t == 0 and hc != turn):
                        continue
                    q = 2 * t - 1 + turn if t else 0
                    b = 2 * q + hc
                    block = arrive(q, hc, p)
                    if t > 1 or (t == 1 and hc == turn):
                        block = block + landed(turn, t - 1, hc, p)
                    ubuf[b, piece_rows(p)] = block
                    copy(ubuf.at[b, piece_rows(p)], zrecv.at[turn, t, hc, p],
                         zsend_sem.at[turn, min(t, 1)], zrecv_sem.at[turn, t, hc, p], sides[turn]).start()

    def pass_on(t, turn, hc, p):
        if t == top - 1 and hc != turn:
            return
        src = 2 * t - 1 + turn if t else 0
        dst = min(2 * t + 1 + turn, nz - 1)
        r = piece_rows(p)
        copy(gat.at[src, hc, r], gat.at[dst, hc, r], gzsend_sem.at[turn, min(top - 1 - t, 1)],
             gzrecv_sem.at[dst, hc, p], sides[turn]).start()

    def hand_over(slot, hc):
        copy(gat.at[slot, hc, piece_rows(0)], gat.at[slot, hc, pl.ds(0, part_rows)],
             gysend_sem, gyrecv_sem.at[slot, hc], other).start()

    lax.fori_loop(0, 2, functools.partial(grad_block, made=True), 0)
    ring(0, (1, 2))
    lax.fori_loop(2, 6, grad_block, 0)
    ring(0, (0,))
    ring(1, (1, 2), (False,))
    for t in range(1, top):
        if t == 1:
            ring(t, (1, 2), (True,))
            ring(t, (0,))
        else:
            ring(t, (1, 2, 0) if t < top - 1 else (1, 0, 2))
        if t < top - 1:
            lax.fori_loop(4 * t + 2, 4 * t + (6 if t < top - 2 else 8), grad_block, 0)
        if t == top - 2:
            hat_1()
    own = 2 * nz - 2

    def trade(p):
        for hc in range(2):
            block = arrive(nz - 1, hc, p)
            ubuf[own + hc, piece_rows(p)] = block + landed(0, top - 1, hc, p) + landed(1, top - 1, hc, p)
            copy(ubuf.at[own + hc, piece_rows(p)], brecv.at[hc, p - 1], bsend_sem, brecv_sem.at[hc, p - 1], other).start()

    def traded(p):
        for hc in range(2):
            wait_bytes(brecv.at[hc, p - 1], brecv_sem.at[hc, p - 1])
            gat[0, hc, piece_rows(p)] = ubuf[own + hc, piece_rows(p)] + brecv[hc, p - 1]
            for turn in range(2):
                pass_on(0, turn, hc, p)

    trade(1)
    for hc in range(2):
        gat[0, hc, piece_rows(0)] = arrive(nz - 1, hc, 0) + landed(0, top - 1, hc, 0) + landed(1, top - 1, hc, 0)
        for turn in range(2):
            pass_on(0, turn, hc, 0)
        hand_over(0, hc)
    traded(1)
    trade(2)
    hat_2()
    traded(2)

    wait_bytes(yrecv, ysend_sem)
    for turn in range(2):
        wait_bytes(zrecv.at[turn, 0, turn], zsend_sem.at[turn, 0])
        wait_bytes(zrecv.at[turn, pl.ds(1, top - 1)], zsend_sem.at[turn, 1])
    wait_bytes(brecv, bsend_sem)
    low = pl.ds(pl.multiple_of(y * part_rows, part_rows), part_rows)
    high = pl.ds(pl.multiple_of((1 - y) * part_rows, part_rows), part_rows)
    rest = pl.ds(2 * part_rows, 2 * part_rows)

    def finish(b, _):
        slot = b // 2
        hc = lax.rem(b, 2)
        far = (slot + 1) // 2
        c = span(jnp.where(lax.rem(slot, 2) == 1, nz - far, far), hc)
        wait_bytes(gat.at[slot, hc, pl.ds(0, part_rows)], gyrecv_sem.at[slot, hc])
        places = ((low, pl.ds(part_rows, part_rows)), (high, pl.ds(0, part_rows)), (rest, rest))
        wide = [sp_ref[here, c].astype(F32) for here, _ in places]
        square = sum(jnp.sum(w * w, axis=0, keepdims=True) for w in wide)
        inverse = 1.0 / jnp.sqrt(square + EPS)
        units = [w * inverse for w in wide]
        grads = [gat[slot, hc, there] for _, there in places]
        along = sum(jnp.sum(u * g, axis=0, keepdims=True) for u, g in zip(units, grads))
        for (here, _), u, g in zip(places, units, grads):
            pg_ref[here, c] = (g - u * along) * inverse
        return 0

    hat_3()
    later = {0: hat_4, 1: hat_5, 2: hat_6}
    for t in range(top):
        for p in range(3):
            for hc in range(2):
                for turn in range(2):
                    if t == top - 1 and hc != turn:
                        continue
                    slot = min(2 * t + 1 + turn, nz - 1)
                    wait_bytes(gat.at[slot, hc, piece_rows(p)], gzrecv_sem.at[slot, hc, p])
                    if t < top - 1:
                        pass_on(t + 1, turn, hc, p)
                    if p == 0:
                        hand_over(slot, hc)
        if t == 0:
            lax.fori_loop(0, 2, finish, 0)
        else:
            lax.fori_loop(4 * t - 2, 4 * t + 2, finish, 0)
        if t in later:
            later[t]()
    lax.fori_loop(2 * nz - 2, 2 * nz, finish, 0)

    for turn in range(2):
        wait_bytes(zrecv.at[turn, 0, turn], gzsend_sem.at[turn, 0])
        wait_bytes(zrecv.at[turn, pl.ds(1, top - 1)], gzsend_sem.at[turn, 1])
    wait_bytes(yrecv, gysend_sem)
    wait_bytes(h1, hsend_sem.at[0])
    wait_bytes(h2, hsend_sem.at[1])
    wait_bytes(h3.at[1], hsend_sem.at[2])
    wait_bytes(h2, hsend_sem.at[3])
    wait_bytes(h1, hsend_sem.at[4])
    for rnd in range(ROUNDS):
        for hf in range(2):
            wait_bytes(crecv.at[rnd, hf], csend_sem.at[rnd, hf])
    for slot in range(ROUNDS + 1):
        wait_bytes(rrecv.at[slot], rsend_sem.at[slot])


def fused(n_dp, n_pr, sf, tf, sp, tp):
    rows, dim = sf.shape
    cols = tp.shape[1]
    width = cols // n_dp
    blocks = rows // 128
    nz, nx = n_dp // 2, n_pr // 4
    quarter = dim // 4
    vmem = pl.BlockSpec(memory_space=pltpu.VMEM)
    anywhere = pl.BlockSpec(memory_space=pl.ANY)
    dma = pltpu.SemaphoreType.DMA
    return pl.pallas_call(
        functools.partial(kernel, n_dp, n_pr),
        out_shape=(
            pltpu.VMEM((dim, cols), F32),
            pltpu.VMEM((rows, dim), F32),
        ),
        in_specs=[anywhere] * 4,
        out_specs=[vmem] * 2,
        scratch_shapes=[
            pltpu.VMEM((rows, dim), BF16),
            pltpu.VMEM((rows, dim), BF16),
            pltpu.VMEM((dim, cols), BF16),
            pltpu.VMEM((dim, cols), BF16),
            pltpu.VMEM((2, dim, width), BF16),
            pltpu.VMEM((rows, cols), F32),
            pltpu.VMEM((rows, dim), BF16),
            pltpu.VMEM((rows, dim), BF16),
            pltpu.VMEM((rows, 128), F32),
            pltpu.VMEM((8, cols), F32),
            pltpu.VMEM((rows, 128), F32),
            pltpu.VMEM((rows, 128), F32),
            pltpu.VMEM((2, rows, width), F32),
            pltpu.VMEM((ROUNDS, cols // 128, 128), F32),
            pltpu.VMEM((ROUNDS, 2, n_dp - 1, cols // 256, 128), F32),
            pltpu.VMEM((ROUNDS + 1, blocks, 128), F32),
            pltpu.VMEM((ROUNDS + 1, n_pr - 1, blocks, 128), F32),
            pltpu.VMEM((dim, rows), BF16),
            pltpu.VMEM((dim, cols), BF16),
            pltpu.VMEM((rows, 128), F32),
            pltpu.VMEM((rows, width), BF16),
            pltpu.VMEM((rows, dim), F32),
            pltpu.VMEM((n_dp, dim, width), F32),
            pltpu.VMEM((n_dp, quarter, width), F32),
            pltpu.VMEM((2, nz // 2, 2, 3, quarter, width), F32),
            pltpu.VMEM((2, 2, quarter, width), F32),
            pltpu.VMEM((nz, 2, dim, width), F32),
            pltpu.VMEM((rows // 2, dim), F32),
            pltpu.VMEM((nx - 1, rows // 2 // nx, dim), F32),
            pltpu.VMEM((2, rows // 2 // nx, dim), F32),
            dma((ROUNDS, 2)), dma((ROUNDS, 2)),
            dma((ROUNDS + 1,)), dma((ROUNDS + 1,)),
            dma, dma((n_dp,)), dma((2, 2)), dma((2, nz // 2, 2, 3)), dma, dma((2, 2)),
            dma((2, 2)), dma((nz, 2, 3)), dma, dma((nz, 2)), dma((5,)), dma((5,)), dma((4,)),
        ],
        compiler_params=pltpu.CompilerParams(
            collective_id=0, has_side_effects=True, vmem_limit_bytes=56 * 1024 * 1024
        ),
    )(sf, tf, sp, tp)


def solution(mesh):
    in_specs = (P("dp", None), P("dp", None), P(None, "proto"), P(None, "proto"))
    out_specs = (P(None, "proto"), P("dp", None))
    return jax.shard_map(
        functools.partial(fused, mesh.shape["dp"], mesh.shape["proto"]),
        mesh=mesh, in_specs=in_specs, out_specs=out_specs, check_vma=False,
    )
```

profile of v0, /device:TPU:8, one launch (start us, length us, event | category | flops | bytes accessed | tf_op | source)
XLA Modules:
  0.0 126.8 jit_solution(16864501342162860617)
XLA Ops:
  0.6 123.2 %shard_map.59 = (f32[256,4096]{1,0:T(8,128)S(1)}, f32[1024,256]{1,0:T(8,128)S(1)}) custom-call(bf16[1024,256]{1,0:T(8,128)(2,1)} %sf_in.1, bf16[1024,256]{1,0:T(8,128)(2,1)} %tf_in.1, bf16[256,4096]{1,0:T(8,128)(2,1)} %sp_in.1, bf16[256,4096]{1,0:T(8,128)(2,1)} %tp_in.1), custom_call_target="tpu_custom_call" | custom-call | tf_op jit(solution)/shard_map/pallas_call | solution.py:520
  123.8 2.0 %copy.8 = f32[256,4096]{1,0:T(8,128)} copy(f32[256,4096]{1,0:T(8,128)S(1)} %get-tuple-element.2) | data formatting | bytes 8388608
  125.8 1.0 copy.9
where the time goes:
time: 127 us
  Pallas kernels  123 us (97%)
  local copies, waits for them, and re-layouts  2.99 us (2%)
    pallas_call x1, Pallas kernels, fused(): pl.pallas_call(functools.partial(kernel, n_dp, n_pr), out_shape=(pltpu.VM...  123 us
    unnamed x2, local copies, waits for them, and re-layouts  2.99 us

commit v1 on v0

--- a/solution.py
+++ b/solution.py
@@ -67,9 +67,15 @@
 
     loads = [
         pltpu.make_async_copy(src, dst, in_sem.at[k])
-        for k, (src, dst) in enumerate(((tf_in, tf_ref), (tp_in, tp_ref), (sf_in, sf_ref), (sp_in, sp_ref)))
+        for k, (src, dst) in enumerate((
+            (tf_in, tf_ref),
+            (tp_in.at[:, pl.ds(0, cols // 2)], tp_ref.at[:, pl.ds(0, cols // 2)]),
+            (tp_in.at[:, pl.ds(cols // 2, cols // 2)], tp_ref.at[:, pl.ds(cols // 2, cols // 2)]),
+            (sf_in, sf_ref),
+            (sp_in, sp_ref),
+        ))
     ]
-    for load in loads:
+    for load in loads[:3]:
         load.start()
     barrier = pltpu.get_barrier_semaphore()
 
@@ -102,6 +108,9 @@
     loads[0].wait()
     lax.fori_loop(0, blocks, norm_rows, 0)
     loads[1].wait()
+    loads[2].wait()
+    for load in loads[3:]:
+        load.start()
     tiles = width // 128
     half_tiles = n_dp * tiles // 2
 
@@ -147,14 +156,14 @@
         return 0
 
     wts[0] = teacher_unit(0)
-    lax.fori_loop(0, n_dp // 2, first_cols, 0, unroll=4)
+    lax.fori_loop(0, n_dp // 2, first_cols, 0, unroll=8)
     pl.semaphore_wait(barrier, n_dp + n_pr - 2)
     send_cols(0, 0)
-    lax.fori_loop(n_dp // 2, n_dp, first_cols, 0, unroll=4)
+    lax.fori_loop(n_dp // 2, n_dp, first_cols, 0, unroll=8)
     send_cols(0, 1)
-    loads[2].wait()
+    loads[3].wait()
     lax.fori_loop(0, blocks, norm_student, 0)
-    loads[3].wait()
+    loads[4].wait()
 
     part[...] = jnp.zeros_like(part)
 
@@ -559,7 +568,7 @@
             dma((ROUNDS, 2)), dma((ROUNDS, 2)),
             dma((ROUNDS + 1,)), dma((ROUNDS + 1,)),
             dma, dma((n_dp,)), dma((2, 2)), dma((2, nz // 2, 2, 3)), dma, dma((2, 2)),
-            dma((2, 2)), dma((nz, 2, 3)), dma, dma((nz, 2)), dma((5,)), dma((5,)), dma((4,)),
+            dma((2, 2)), dma((nz, 2, 3)), dma, dma((nz, 2)), dma((5,)), dma((5,)), dma((5,)),
         ],
         compiler_params=pltpu.CompilerParams(
             collective_id=0, has_side_effects=True, vmem_limit_bytes=56 * 1024 * 1024
@@ -567,10 +576,36 @@
     )(sf, tf, sp, tp)
 
 
+def drain(parts, pg_ref, fg_ref, pg_out, fg_out, sem):
+    copies = []
+    for src, dst in ((pg_ref, pg_out), (fg_ref, fg_out)):
+        step = src.shape[0] // parts
+        for k in range(parts):
+            r = pl.ds(k * step, step)
+            copies.append(pltpu.make_async_copy(src.at[r], dst.at[r], sem.at[len(copies)]))
+    for copy in copies:
+        copy.start()
+    for copy in copies:
+        copy.wait()
+
+
+def step(n_dp, n_pr, sf, tf, sp, tp):
+    pg, fg = fused(n_dp, n_pr, sf, tf, sp, tp)
+    parts = 4
+    return pl.pallas_call(
+        functools.partial(drain, parts),
+        out_shape=(jax.ShapeDtypeStruct(pg.shape, F32), jax.ShapeDtypeStruct(fg.shape, F32)),
+        in_specs=[pl.BlockSpec(memory_space=pltpu.VMEM)] * 2,
+        out_specs=[pl.BlockSpec(memory_space=pl.ANY)] * 2,
+        scratch_shapes=[pltpu.SemaphoreType.DMA((2 * parts,))],
+        compiler_params=pltpu.CompilerParams(vmem_limit_bytes=16 * 1024 * 1024),
+    )(pltpu.with_memory_space_constraint(pg, pltpu.VMEM), pltpu.with_memory_space_constraint(fg, pltpu.VMEM))
+
+
 def solution(mesh):
     in_specs = (P("dp", None), P("dp", None), P(None, "proto"), P(None, "proto"))
     out_specs = (P(None, "proto"), P("dp", None))
     return jax.shard_map(
-        functools.partial(fused, mesh.shape["dp"], mesh.shape["proto"]),
+        functools.partial(step, mesh.shape["dp"], mesh.shape["proto"]),
         mesh=mesh, in_specs=in_specs, out_specs=out_specs, check_vma=False,
     )

time: 127 us -> 126 us (level)
  Pallas kernels: 123 us -> 126 us
  local copies, waits for them, and re-layouts: 2.99 us -> 0 us
    unnamed x2 -> x0, local copies, waits for them, and re-layouts: 2.99 us -> none
    pallas_call x0 -> x1, Pallas kernels: none -> 2.39 us  [step(): pl.pallas_call(functools.partial(drain, parts), out_shape=(jax.ShapeDtype...]
where the time goes in v1:
time: 126 us
  Pallas kernels  126 us (100%)
    pallas_call x1, Pallas kernels, fused(): pl.pallas_call(functools.partial(kernel, n_dp, n_pr), out_shape=(pltpu.VM...  123 us

profile of v1, /device:TPU:8, one launch (start us, length us, event | category | flops | bytes accessed | tf_op | source)
XLA Modules:
  0.0 126.2 jit_solution(14609653280258533518)
XLA Ops:
  0.6 123.2 %shard_map.59 = (f32[256,4096]{1,0:T(8,128)S(1)}, f32[1024,256]{1,0:T(8,128)S(1)}) custom-call(bf16[1024,256]{1,0:T(8,128)(2,1)} %sf_in.1, bf16[1024,256]{1,0:T(8,128)(2,1)} %tf_in.1, bf16[256,4096]{1,0:T(8,128)(2,1)} %sp_in.1, bf16[256,4096]{1,0:T(8,128)(2,1)} %tp_in.1), custom_call_target="tpu_custom_call" | custom-call | tf_op jit(solution)/shard_map/pallas_call | solution.py:529
  123.8 2.4 %shard_map.60 = (f32[256,4096]{1,0:T(8,128)}, f32[1024,256]{1,0:T(8,128)}) custom-call(f32[256,4096]{1,0:T(8,128)S(1)} %get-tuple-element.4.pg_ref, f32[1024,256]{1,0:T(8,128)S(1)} %get-tuple-element.5.fg_ref), custom_call_target="tpu_custom_call" | custom-call | tf_op jit(solution)/shard_map/pallas_call | solution.py:595

commit v2 on v1

--- a/solution.py
+++ b/solution.py
@@ -112,7 +112,7 @@
     for load in loads[3:]:
         load.start()
     tiles = width // 128
-    half_tiles = n_dp * tiles // 2
+    cuts = (0, n_dp // 4, 3 * n_dp // 4, n_dp)
 
     def hops(j, n):
         return min(j, n - j)
@@ -125,10 +125,10 @@
         key=lambda o: -(2 * hops(o[0], nx) + 4 * o[1] + o[2]))
 
     def send_cols(rnd, hf):
-        r = pl.ds(hf * half_tiles, half_tiles)
+        r = pl.ds(cuts[hf] * tiles, (cuts[hf + 1] - cuts[hf]) * tiles)
         for slot, (a, j) in enumerate(dp_peers):
             pltpu.make_async_remote_copy(
-                src_ref=csend.at[rnd, r], dst_ref=crecv.at[rnd, hf, slot],
+                src_ref=csend.at[rnd, r], dst_ref=crecv[hf].at[rnd, slot],
                 send_sem=csend_sem.at[rnd, hf], recv_sem=crecv_sem.at[rnd, hf],
                 device_id={"dp": lax.rem(y + a, 2) * nz + lax.rem(z + j, nz)}, device_id_type=MESH,
             ).start()
@@ -156,11 +156,12 @@
         return 0
 
     wts[0] = teacher_unit(0)
-    lax.fori_loop(0, n_dp // 2, first_cols, 0, unroll=8)
+    lax.fori_loop(0, cuts[1], first_cols, 0, unroll=4)
     pl.semaphore_wait(barrier, n_dp + n_pr - 2)
     send_cols(0, 0)
-    lax.fori_loop(n_dp // 2, n_dp, first_cols, 0, unroll=8)
-    send_cols(0, 1)
+    for hf in range(1, 3):
+        lax.fori_loop(cuts[hf], cuts[hf + 1], first_cols, 0, unroll=4)
+        send_cols(0, hf)
     loads[3].wait()
     lax.fori_loop(0, blocks, norm_student, 0)
     loads[4].wait()
@@ -185,10 +186,12 @@
         lax.fori_loop(lo, hi, body, 0)
 
     def receive_v(rnd, hf):
-        wait_bytes(crecv.at[rnd, hf], crecv_sem.at[rnd, hf])
-        v = 1.0 / (csend[rnd, pl.ds(hf * half_tiles, half_tiles), :] + jnp.sum(crecv[rnd, hf], axis=0))
-        for t in range(half_tiles):
-            lanes = slice((hf * half_tiles + t) * 128, (hf * half_tiles + t + 1) * 128)
+        wait_bytes(crecv[hf].at[rnd], crecv_sem.at[rnd, hf])
+        count = (cuts[hf + 1] - cuts[hf]) * tiles
+        base = cuts[hf] * tiles
+        v = 1.0 / (csend[rnd, pl.ds(base, count), :] + jnp.sum(crecv[hf][rnd], axis=0))
+        for t in range(count):
+            lanes = slice((base + t) * 128, (base + t + 1) * 128)
             vb[:, lanes] = jnp.broadcast_to(v[t:t + 1, :], (8, 128))
 
     def lane_sums(slot, acc):
@@ -216,19 +219,19 @@
         def body(k, _):
             r = pl.ds(pl.multiple_of(k * 128, 128), 128)
             acc = racc[r, :].reshape(16, 8, 128) if hf else jnp.zeros((16, 8, 128), F32)
-            for t in range(hf * half_tiles, (hf + 1) * half_tiles):
+            for t in range(cuts[hf] * tiles, cuts[hf + 1] * tiles):
                 e = expo[r, t * 128:(t + 1) * 128].reshape(16, 8, 128)
                 acc = acc + e * vb[:, t * 128:(t + 1) * 128][None]
             racc[r, :] = acc.reshape(128, 128)
             return 0
 
         lax.fori_loop(0, blocks, body, 0)
-        if hf:
+        if hf == len(cuts) - 2:
             lane_sums(rnd, racc)
 
     def col_pass(rnd, hf):
         def body(i, _):
-            k = hf * (n_dp // 2) + i
+            k = cuts[hf] + i
             c = pl.ds(pl.multiple_of(k * width, width), width)
 
             def inner(b, acc):
@@ -242,7 +245,7 @@
             put_cols(rnd, k, jnp.sum(jnp.concatenate(acc, axis=1), axis=0, keepdims=True))
             return 0
 
-        lax.fori_loop(0, n_dp // 2, body, 0)
+        lax.fori_loop(0, cuts[hf + 1] - cuts[hf], body, 0)
 
     def span(rel, hc):
         chunk = lax.rem(z + rel, nz)
@@ -271,8 +274,9 @@
             student(2 * share, 3 * share)
         receive_v(rnd, 0)
         row_pass(rnd, 0)
-        receive_v(rnd, 1)
-        row_pass(rnd, 1)
+        for hf in range(1, 3):
+            receive_v(rnd, hf)
+            row_pass(rnd, hf)
         send_rows(rnd)
         if rnd == 0:
             student(share, 2 * share)
@@ -290,8 +294,9 @@
             widen(u, ub)
             col_pass(rnd + 1, 0)
             send_cols(rnd + 1, 0)
-            col_pass(rnd + 1, 1)
-            send_cols(rnd + 1, 1)
+            for hf in range(1, 3):
+                col_pass(rnd + 1, hf)
+                send_cols(rnd + 1, hf)
         else:
             widen(u * factor, ub)
     def copy(src, dst, send, recv, to):
@@ -510,8 +515,8 @@
     wait_bytes(h2, hsend_sem.at[3])
     wait_bytes(h1, hsend_sem.at[4])
     for rnd in range(ROUNDS):
-        for hf in range(2):
-            wait_bytes(crecv.at[rnd, hf], csend_sem.at[rnd, hf])
+        for hf in range(len(cuts) - 1):
+            wait_bytes(crecv[hf].at[rnd], csend_sem.at[rnd, hf])
     for slot in range(ROUNDS + 1):
         wait_bytes(rrecv.at[slot], rsend_sem.at[slot])
 
@@ -549,7 +554,11 @@
             pltpu.VMEM((rows, 128), F32),
             pltpu.VMEM((2, rows, width), F32),
             pltpu.VMEM((ROUNDS, cols // 128, 128), F32),
-            pltpu.VMEM((ROUNDS, 2, n_dp - 1, cols // 256, 128), F32),
+            [
+                pltpu.VMEM((ROUNDS, n_dp - 1, cols // 512, 128), F32),
+                pltpu.VMEM((ROUNDS, n_dp - 1, cols // 256, 128), F32),
+                pltpu.VMEM((ROUNDS, n_dp - 1, cols // 512, 128), F32),
+            ],
             pltpu.VMEM((ROUNDS + 1, blocks, 128), F32),
             pltpu.VMEM((ROUNDS + 1, n_pr - 1, blocks, 128), F32),
             pltpu.VMEM((dim, rows), BF16),
@@ -565,7 +574,7 @@
             pltpu.VMEM((rows // 2, dim), F32),
             pltpu.VMEM((nx - 1, rows // 2 // nx, dim), F32),
             pltpu.VMEM((2, rows // 2 // nx, dim), F32),
-            dma((ROUNDS, 2)), dma((ROUNDS, 2)),
+            dma((ROUNDS, 3)), dma((ROUNDS, 3)),
             dma((ROUNDS + 1,)), dma((ROUNDS + 1,)),
             dma, dma((n_dp,)), dma((2, 2)), dma((2, nz // 2, 2, 3)), dma, dma((2, 2)),
             dma((2, 2)), dma((nz, 2, 3)), dma, dma((nz, 2)), dma((5,)), dma((5,)), dma((5,)),

time: 126 us -> 127 us (level)
  no operation moved by 1% of the time
where the time goes in v2:
time: 127 us
  Pallas kernels  126 us (99%)
    pallas_call x1, Pallas kernels, fused(): pl.pallas_call(functools.partial(kernel, n_dp, n_pr), out_shape=(pltpu.VM...  123 us

profile of v2, /device:TPU:8, one launch (start us, length us, event | category | flops | bytes accessed | tf_op | source)
XLA Modules:
  0.0 126.5 jit_solution(963615626732875026)
XLA Ops:
  0.6 123.5 %shard_map.59 = (f32[256,4096]{1,0:T(8,128)S(1)}, f32[1024,256]{1,0:T(8,128)S(1)}) custom-call(bf16[1024,256]{1,0:T(8,128)(2,1)} %sf_in.1, bf16[1024,256]{1,0:T(8,128)(2,1)} %tf_in.1, bf16[256,4096]{1,0:T(8,128)(2,1)} %sp_in.1, bf16[256,4096]{1,0:T(8,128)(2,1)} %tp_in.1), custom_call_target="tpu_custom_call" | custom-call | tf_op jit(solution)/shard_map/pallas_call | solution.py:534
  124.1 2.4 %shard_map.60 = (f32[256,4096]{1,0:T(8,128)}, f32[1024,256]{1,0:T(8,128)}) custom-call(f32[256,4096]{1,0:T(8,128)S(1)} %get-tuple-element.4.pg_ref, f32[1024,256]{1,0:T(8,128)S(1)} %get-tuple-element.5.fg_ref), custom_call_target="tpu_custom_call" | custom-call | tf_op jit(solution)/shard_map/pallas_call | solution.py:604
